TPU v7x, 256 devices: a whole 4x4x8 slice. The times are simulated.
256 devices in a mesh: delay: 8 (over y, core), row: 32 (over x, z).
Axes of the slice: x: 4, y: 4, z: 8, core: 2. Of those that a mesh axis runs over, the one named last changes fastest.
Arguments:
- incident: bfloat16 [3, 16384, 128], P(None, 'row'), may hold values from -6 to 6
- history: float32 [16, 16384, 128], P('delay', 'row'), may hold values from -6 to 6
- couplings: bfloat16 [16, 16384, 2048], P('delay', 'row'), may hold values from -0.06591797 to 0.06591797
- block_inverse: float32 [128, 128, 128], P('row')
- load_coeff: float32 [16384], P('row'), may hold values from 0.02 to 0.2
- pattern: int32 [16, 128, 16], P('delay', 'row'), may hold values from 0 to 63, as said below
- wanted: int32 [32, 32, 2], replicated, may hold values from -1 to 3, as said below
Outputs:
- currents: bfloat16 [3, 16384, 128], P(None, 'row')
- future: float32 [16, 16384, 128], P('delay', 'row')
Inputs may be any that keep to these rules, and one draw needn't show every extreme that they name: wanted[q, p, c] for c below a count is a distinct local block index of row owner p that owner q needs, and -1 after it; every owner needs between 1 and 2 blocks of every owner, and exactly 2 of its own. pattern[l, i, s] over s are 16 distinct slots p * 2 + c whose entry wanted[q, p, c] is not -1, q the row owner of block row i; every such slot of q is named by some row of that owner.
All inputs are finite; a program needn't handle non-finite values.
Results may differ from a plain program's by a relative error of at most 0.009.
Values may be sent and summed in bfloat16 or wider, within the bound.
A program may use at most 64 MiB of HBM per device.

v0:
```python
import jax
import jax.numpy as jnp
from jax import lax
from jax.sharding import PartitionSpec as P

STEPS = 3


def passed_along(value, axis, steps):
    count = lax.axis_size(axis)
    leading, last = (max(0, -steps), min(count, count - steps))
    return lax.ppermute(value, axis, [(source, source + steps) for source in range(leading, last)])


def spread(value, axis, source):
    kept = jnp.where(lax.axis_index(axis) == source, value, 0).astype(value.dtype)
    return lax.psum(kept, axis)


def solve_step(incoming, field, block_inverse, load_coeff):
    blk_rows = block_inverse.shape[0]
    size_blk = block_inverse.shape[1]
    rhs = incoming.astype(jnp.float32) - field
    solved = jnp.einsum(
        "iab,ibc->iac",
        block_inverse,
        rhs.reshape(blk_rows, size_blk, rhs.shape[1]),
        precision=lax.Precision.HIGHEST,
    ).reshape(rhs.shape)
    return (solved - load_coeff[:, None] * solved * solved * solved).astype(jnp.bfloat16)


def local(incident, history, couplings, block_inverse, load_coeff, pattern, wanted):
    blk_rows = block_inverse.shape[0]
    size_blk = block_inverse.shape[1]
    excite = incident.shape[2]
    local_delays = history.shape[0]
    nonzero = couplings.shape[2] // size_blk
    owner = lax.axis_index("row")
    slots = wanted.shape[2]
    zmats = couplings.reshape(local_delays, blk_rows, size_blk, nonzero * size_blk)
    mine = lax.dynamic_index_in_dim(wanted, owner, 0, keepdims=False)
    source_owner = pattern // slots
    source_slot = pattern % slots
    local_block = mine[source_owner, source_slot]
    position = source_owner * blk_rows + jnp.maximum(local_block, 0)
    acc = history
    outputs = []
    for step in range(STEPS):
        nearest = passed_along(acc[0].astype(jnp.bfloat16), "delay", -1).astype(jnp.float32)
        current = solve_step(incident[step], acc[0], block_inverse, load_coeff)
        current = spread(current, "delay", 0)
        blocks = current.reshape(blk_rows, size_blk, excite)
        source = lax.all_gather(blocks, "row", axis=0, tiled=True)
        picked = source[position].reshape(local_delays, blk_rows, nonzero * size_blk, excite)
        products = jnp.einsum("krab,krbc->krac", zmats, picked, preferred_element_type=jnp.float32)
        products = products.reshape(local_delays, blk_rows * size_blk, excite)
        acc = jnp.concatenate([acc[1:], nearest[None]], 0) + products
        outputs.append(current)
    return (jnp.stack(outputs), acc)


def solution(mesh):
    in_specs = (
        P(None, "row", None),
        P("delay", "row", None),
        P("delay", "row", None),
        P("row", None, None),
        P("row"),
        P("delay", "row", None),
        P(),
    )
    out_specs = (P(None, "row", None), P("delay", "row", None))
    return jax.shard_map(local, mesh=mesh, in_specs=in_specs, out_specs=out_specs, check_vma=False)
```

profile of v0, /device:TPU:1, one launch (start us, length us, event | category | flops | bytes accessed | tf_op | source)
XLA Modules:
  0.0 491.4 jit_solution(7382576863162925215)
XLA Ops:
  7.2 0.0 copy-start
  7.2 0.0 copy-start.5
  7.2 0.0 all-reduce.4.cloned.1.call-start
  7.2 1.1 convert_subtract_fusion.2
  8.4 0.4 fusion.16
  8.8 1.5 fusion.8
  10.2 0.0 all-reduce.4.cloned.1.call-update
  10.3 0.0 all-gather.4.cloned.1.call-start
  10.3 66.8 %all-reduce.4.cloned.1.call-done = bf16[512,128]{1,0:T(8,128)(2,1)} async-done(((bf16[512,128]{1,0:T(8,128)(2,1)}), bf16[512,128]{1,0:T(8,128)(2,1)}) %all-reduce.4.cloned.1.call-update) | async-done | bytes 131088 | tf_op jit(solution)/shard_map/psum | solution.py:17
  77.1 0.0 all-gather.4.cloned.1.call-update
  77.1 0.0 all-reduce.6.cloned.1.call-start
  77.2 1.0 fusion.3
  78.2 4.7 collective-permute-start
  82.8 0.7 fusion.11
  83.5 0.1 reshape.78
  83.6 0.7 dynamic-slice_bitcast_fusion
  84.3 1.5 gather_fusion
  85.8 0.1 reshape.118
  85.9 0.1 reshape.86
  86.1 74.2 %all-gather.4.cloned.1.call-done = bf16[128,128,128]{2,1,0:T(8,128)(2,1)} async-done(((bf16[4,128,128]{2,1,0:T(8,128)(2,1)}), bf16[128,128,128]{2,1,0:T(8,128)(2,1)}) %all-gather.4.cloned.1.call-update) | async-done | bytes 4194320 | tf_op jit(solution)/shard_map/all_gather | solution.py:54
  160.3 5.3 %gather_fusion.1 = bf16[128,128,128]{2,1,0:T(8,128)(2,1)} fusion(bf16[128,128,128]{2,1,0:T(8,128)(2,1)} %all-gather.4.cloned.1.call-done, s32[1024]{0:T(1024)S(1)} %pad_clamp_fusion), kind=kCustom, calls=%fused_computation.1 | custom fusion | bytes 8389120 | tf_op jit(solution)/shard_map/gather | solution.py:55
  165.6 4.7 fusion.19
  170.3 0.1 maximum_add_fusion
  170.5 0.4 fusion.17
  170.9 0.8 fusion.7
  171.7 0.0 all-reduce.6.cloned.1.call-update
  171.7 0.0 all-gather.6.cloned.1.call-start
  171.7 62.4 %all-reduce.6.cloned.1.call-done = bf16[512,128]{1,0:T(8,128)(2,1)} async-done(((bf16[512,128]{1,0:T(8,128)(2,1)}), bf16[512,128]{1,0:T(8,128)(2,1)}) %all-reduce.6.cloned.1.call-update) | async-done | bytes 131088 | tf_op jit(solution)/shard_map/psum | solution.py:17
  234.1 0.0 all-gather.6.cloned.1.call-update
  234.1 0.0 all-reduce.8.cloned.1.call-start
  234.2 4.7 collective-permute-start.1
  238.9 1.6 collective-permute-done.1
  240.5 76.3 %all-gather.6.cloned.1.call-done = bf16[128,128,128]{2,1,0:T(8,128)(2,1)} async-done(((bf16[4,128,128]{2,1,0:T(8,128)(2,1)}), bf16[128,128,128]{2,1,0:T(8,128)(2,1)}) %all-gather.6.cloned.1.call-update) | async-done | bytes 4194320 | tf_op jit(solution)/shard_map/all_gather | solution.py:54
  316.8 5.3 %gather_fusion.2 = bf16[128,128,128]{2,1,0:T(8,128)(2,1)} fusion(bf16[128,128,128]{2,1,0:T(8,128)(2,1)} %all-gather.6.cloned.1.call-done, s32[1024]{0:T(1024)S(1)} %pad_clamp_fusion), kind=kCustom, calls=%fused_computation.2 | custom fusion | bytes 8389120 | tf_op jit(solution)/shard_map/gather | solution.py:55
  322.1 4.7 fusion.20
  326.8 0.1 maximum_add_fusion.1
  327.0 0.4 fusion.18
  327.4 0.8 fusion.6
  328.2 0.0 all-reduce.8.cloned.1.call-update
  328.2 0.0 all-gather.8.cloned.1.call-start
  328.2 62.4 %all-reduce.8.cloned.1.call-done = bf16[512,128]{1,0:T(8,128)(2,1)} async-done(((bf16[512,128]{1,0:T(8,128)(2,1)}), bf16[512,128]{1,0:T(8,128)(2,1)}) %all-reduce.8.cloned.1.call-update) | async-done | bytes 131088 | tf_op jit(solution)/shard_map/psum | solution.py:17
  390.6 0.0 all-gather.8.cloned.1.call-update
  390.7 4.7 collective-permute-start.2
  395.4 1.7 pad_maximum_fusion
  397.1 76.6 %all-gather.8.cloned.1.call-done = bf16[128,128,128]{2,1,0:T(8,128)(2,1)} async-done(((bf16[4,128,128]{2,1,0:T(8,128)(2,1)}), bf16[128,128,128]{2,1,0:T(8,128)(2,1)}) %all-gather.8.cloned.1.call-update) | async-done | bytes 4194320 | tf_op jit(solution)/shard_map/all_gather | solution.py:54
  473.7 5.3 %gather_fusion.3 = bf16[128,128,128]{2,1,0:T(8,128)(2,1)} fusion(bf16[128,128,128]{2,1,0:T(8,128)(2,1)} %all-gather.8.cloned.1.call-done, s32[1024]{0:T(1024)S(1)} %pad_clamp_fusion), kind=kCustom, calls=%fused_computation.3 | custom fusion | bytes 8389120 | tf_op jit(solution)/shard_map/gather | solution.py:55
  478.9 4.7 fusion.21
  483.7 0.9 maximum_add_fusion.2
  (22 shorter events, 0.2 us)
Async XLA Ops:
  7.2 1.2 copy-start
  7.2 78.7 %copy-start.5 = (s32[2,4,16]{2,1,0:T(4,128)S(1)}, s32[2,4,16]{2,1,0:T(4,128)}, u32[]{:S(2)}) copy-start(s32[2,4,16]{2,1,0:T(4,128)} %param.12) | copy-start | bytes 1540
  7.2 69.9 %all-reduce.4.cloned.1.call-start = ((), (), s32[]{:S(2)}) async-start(), calls=%async_computation | async-start | bytes 262144 | tf_op jit(solution)/shard_map/psum | solution.py:17
  10.3 150.0 %all-gather.4.cloned.1.call-start = ((), (), s32[]{:S(2)}) async-start(), calls=%async_computation.1 | async-start | bytes 4325376 | tf_op jit(solution)/shard_map/all_gather | solution.py:54
  77.1 157.0 %all-reduce.6.cloned.1.call-start = ((), (), s32[]{:S(2)}) async-start(), calls=%async_computation.2 | async-start | bytes 262144 | tf_op jit(solution)/shard_map/psum | solution.py:17
  78.2 7.9 %collective-permute-start = (bf16[512,128]{1,0:T(8,128)(2,1)S(1)}, bf16[512,128]{1,0:T(8,128)(2,1)S(1)}, u32[]{:S(2)}, u32[]{:S(2)}) collective-permute-start(bf16[512,128]{1,0:T(8,128)(2,1)S(1)} %fusion.3), channel_id=1, source_target_pairs={{32,0},{64,32},{96,64},{128,96},{160,128},{192,160},{224,192},{33,... | collective-permute-start | bytes 393224 | tf_op jit(solution)/shard_map/ppermute | solution.py:12
  165.6 4.8 copy-start.3
  165.6 5.3 %copy-start.4 = (f32[512]{0:T(512)S(1)}, f32[512]{0:T(512)}, u32[]{:S(2)}) copy-start(f32[512]{0:T(512)} %param.11) | copy-start | bytes 6148
  171.7 145.1 %all-gather.6.cloned.1.call-start = ((), (), s32[]{:S(2)}) async-start(), calls=%async_computation.3 | async-start | bytes 4325376 | tf_op jit(solution)/shard_map/all_gather | solution.py:54
  234.1 156.5 %all-reduce.8.cloned.1.call-start = ((), (), s32[]{:S(2)}) async-start(), calls=%async_computation.4 | async-start | bytes 262144 | tf_op jit(solution)/shard_map/psum | solution.py:17
  234.2 6.3 %collective-permute-start.1 = (bf16[512,128]{1,0:T(8,128)(2,1)S(1)}, bf16[512,128]{1,0:T(8,128)(2,1)S(1)}, u32[]{:S(2)}, u32[]{:S(2)}) collective-permute-start(bf16[512,128]{1,0:T(8,128)(2,1)S(1)} %fusion.4), channel_id=1, source_target_pairs={{32,0},{64,32},{96,64},{128,96},{160,128},{192,160},{224,192},{33,... | collective-permute-start | bytes 393224 | tf_op jit(solution)/shard_map/ppermute | solution.py:12
  326.8 68.5 %copy-start.1 = (bf16[512,128]{1,0:T(8,128)(2,1)S(1)}, bf16[512,128]{1,0:T(8,128)(2,1)}, u32[]{:S(2)}) copy-start(bf16[512,128]{1,0:T(8,128)(2,1)} %all-reduce.4.cloned.1.call-done) | copy-start | bytes 393220
  326.8 68.5 %copy-start.2 = (bf16[512,128]{1,0:T(8,128)(2,1)S(1)}, bf16[512,128]{1,0:T(8,128)(2,1)}, u32[]{:S(2)}) copy-start(bf16[512,128]{1,0:T(8,128)(2,1)} %all-reduce.6.cloned.1.call-done) | copy-start | bytes 393220
  328.2 145.5 %all-gather.8.cloned.1.call-start = ((), (), s32[]{:S(2)}) async-start(), calls=%async_computation.5 | async-start | bytes 4325376 | tf_op jit(solution)/shard_map/all_gather | solution.py:54
  390.7 6.4 %collective-permute-start.2 = (bf16[512,128]{1,0:T(8,128)(2,1)S(1)}, bf16[512,128]{1,0:T(8,128)(2,1)S(1)}, u32[]{:S(2)}, u32[]{:S(2)}) collective-permute-start(bf16[512,128]{1,0:T(8,128)(2,1)S(1)} %fusion.5), channel_id=1, source_target_pairs={{32,0},{64,32},{96,64},{128,96},{160,128},{192,160},{224,192},{33,... | collective-permute-start | bytes 393224 | tf_op jit(solution)/shard_map/ppermute | solution.py:12
Sparse Core Ops, SparseCore 0:
  10.9 66.1 all-reduce.3
  80.0 80.2 all-gather.3
  171.8 62.2 all-reduce.5
  236.6 80.2 all-gather.5
  328.3 62.2 all-reduce.7
  393.4 80.2 all-gather.7
where the time goes:
time: 494 us; the launch traced here: 491 us
  waiting for transfers between devices  420 us (85%)
  local copies, waits for them, and re-layouts  19.3 us (4%)
  matrix products  15.3 us (3%)
  starting transfers between devices  14.3 us (3%)
  between operations  14.3 us (3%)
  other arithmetic  7.82 us (2%)
    all_gather x3, waiting for transfers between devices, local(): source = lax.all_gather(blocks, 'row', axis=0, tiled=True)  227 us
    psum x3, waiting for transfers between devices, spread(): return lax.psum(kept, axis)  192 us
    gather x3, local copies, waits for them, and re-layouts, local(): source[position].reshape(local_delays, blk_rows, nonzero * size_blk, excite)  15.8 us
    dot_general x3, matrix products, local(): jnp.einsum('krab,krbc->krac', zmats, picked, preferred_element_type=jnp.f...  14.2 us
    ppermute x3, starting transfers between devices, passed_along(): lax.ppermute(value, axis, [(source, source + steps) for source in range(l...  14 us
  transfers between devices with their start and end apart: 9, of which 7 were waited for; matrix products, arithmetic and copies ran while one was open for 1% of the time, Pallas kernels for 0%

commit v1 on v0

v1 whole, which is shorter than its diff:
```python
import jax
import jax.numpy as jnp
from jax import lax
from jax.experimental import pallas as pl
from jax.experimental.pallas import tpu as pltpu
from jax.sharding import PartitionSpec as P

STEPS = 3
NX, NY, NZ = 4, 4, 8
PIECES = 2 * NY
BLK = 4
CAP = 2
GROUP = NZ * CAP
SLOTS = NX * GROUP
PICKS = 16
TOGETHER = 4
BF16, F32 = jnp.bfloat16, jnp.float32
HIGHEST = lax.Precision.HIGHEST


def kernel(
    inc_hbm, hist_hbm, z_hbm, binv_hbm, lc_ref, pat, sel, cur_hbm, fut_hbm,
    inc, acc, zmat, binv, outv, pass_out, pass_in, cut, staged, *rest,
):
    zblk, got = rest[:STEPS], rest[STEPS : 2 * STEPS]
    (
        local_sem, out_sem, pass_ss, pass_rs, cut_ss, cut_rs, z_ss, z_rs, x_ss, x_rs,
        up_ss, up_rs, down_ss, down_rs, fwd_ss, fwd_rs, core_ss, core_rs,
    ) = rest[2 * STEPS :]
    d, q = lax.axis_index("delay"), lax.axis_index("row")
    y, k = d // 2, d % 2
    x, z = q // NZ, q % NZ
    rows = PIECES * 16
    up, down, far = (lax.rem(y + s, NY) * 2 + k for s in (1, NY - 1, 2))
    other = y * 2 + 1 - k
    sent = []

    def remote(src, dst, ss, rs, dd, qq):
        return pltpu.make_async_remote_copy(
            src_ref=src, dst_ref=dst, send_sem=ss, recv_sem=rs, device_id=(dd, qq),
            device_id_type=pl.DeviceIdType.MESH,
        )

    def send(*args):
        copy = remote(*args)
        copy.start()
        sent.append(copy)

    loads = [
        pltpu.make_async_copy(hist_hbm, acc, local_sem.at[0]),
        pltpu.make_async_copy(inc_hbm, inc, local_sem.at[1]),
        pltpu.make_async_copy(binv_hbm, binv, local_sem.at[2]),
        pltpu.make_async_copy(z_hbm, zmat, local_sem.at[3]),
    ]
    for load in loads:
        load.start()

    barrier = pltpu.get_barrier_semaphore()
    peers = [(lax.rem(d + s, PIECES), q) for s in range(1, PIECES)]
    peers += [(d, x * NZ + lax.rem(z + s, NZ)) for s in range(1, NZ)]
    peers += [(d, lax.rem(x + s, NX) * NZ + z) for s in range(1, NX)]
    for peer in peers:
        pl.semaphore_signal(barrier, inc=1, device_id=peer, device_id_type=pl.DeviceIdType.MESH)
    loads[0].wait()
    pass_out[0] = acc[0].astype(BF16)

    @pl.when(d == PIECES - 1)
    def _():
        pass_in[...] = jnp.zeros_like(pass_in)

    loads[1].wait()
    loads[2].wait()
    pl.semaphore_wait(barrier, len(peers))

    def passing(n):
        return remote(pass_out.at[n], pass_in.at[n], pass_ss.at[n], pass_rs.at[n], lax.rem(d + PIECES - 1, PIECES), q)

    def scatter(n, e):
        return remote(cut.at[n, e], zblk[n].at[z], cut_ss.at[n, e], cut_rs.at[n], e, q)

    def solve(n):
        for i in range(BLK):
            part = pl.ds(i * rows, rows)
            load = jnp.broadcast_to(lc_ref[pl.ds(i, 1), :], (rows, rows)).T
            rhs = inc[n, part, :].astype(F32) - acc[0, part, :]
            solved = jnp.dot(binv[i], rhs, precision=HIGHEST, preferred_element_type=F32)
            current = (solved - load * solved * solved * solved).astype(BF16)
            cut[n, :, i] = current.reshape(PIECES, 16, rows)

    def product(n, half, i):
        total = None
        for s in range(0, PICKS, TOGETHER):
            picked = [got[n][:, pat[(half * BLK + i) * PICKS + s + t]].reshape(rows, rows) for t in range(TOGETHER)]
            part = jnp.dot(
                zmat[half, pl.ds(pl.multiple_of(i * rows, rows), rows), pl.ds(s * rows, TOGETHER * rows)],
                jnp.concatenate(picked, axis=0),
                preferred_element_type=F32,
            )
            total = part if total is None else total + part
        return total

    def first_product(n):
        def body(i, carry):
            part = pl.ds(pl.multiple_of(i * rows, rows), rows)
            acc[0, part, :] = acc[1, part, :] + product(n, 0, i)
            return carry

        lax.fori_loop(0, BLK, body, 0)

    def second_product(n):
        @pl.when(d < PIECES - 1)
        def _():
            passing(n).wait_recv()

        def body(i, carry):
            part = pl.ds(pl.multiple_of(i * rows, rows), rows)
            acc[1, part, :] = pass_in[n, part, :].astype(F32) + product(n, 1, i)
            return carry

        lax.fori_loop(0, BLK, body, 0)
        outv[n] = got[n][:, pl.ds(SLOTS, BLK)].transpose(1, 0, 2, 3)
        pltpu.make_async_copy(outv.at[n], cur_hbm.at[n], out_sem.at[n]).start()

    for n in range(STEPS):
        zb, g = zblk[n], got[n]

        @pl.when(d == 0)
        def _():
            solve(n)
            for e in range(1, PIECES):
                scatter(n, e).start()
            zb[z] = cut[n, 0]

        @pl.when(d > 0)
        def _():
            passing(n).start()
            scatter(n, 1).wait_recv()

        for s in (4, 3, 5, 2, 6, 1, 7):
            if s < NZ:
                to = lax.rem(z + s, NZ)
                send(zb.at[z], zb.at[z], z_ss.at[n, s], z_rs.at[n, z], d, x * NZ + to)
        if n:
            second_product(n - 1)
        g[d, pl.ds(SLOTS, BLK)] = zb[z]

        chunks = [(SLOTS, BLK)] + [(lax.rem(x + s, NX) * GROUP, GROUP) for s in (0, *[t for t in (1, 3, 2) if t < NX])]
        to_up = [j for j in (1, 3) if j < len(chunks)]

        def chunk(e, j):
            return g.at[e, pl.ds(*chunks[j])]

        def spread(j):
            send(chunk(d, j), chunk(d, j), up_ss.at[n, j], up_rs.at[n, j], up, q)
            send(chunk(d, j), chunk(d, j), down_ss.at[n, j], down_rs.at[n, j], down, q)

        def forward(j):
            remote(chunk(down, j), chunk(down, j), up_ss.at[n, j], up_rs.at[n, j], down, q).wait_recv()
            remote(chunk(up, j), chunk(up, j), down_ss.at[n, j], down_rs.at[n, j], up, q).wait_recv()
            e, to = (down, up) if j in to_up else (up, down)
            send(chunk(e, j), chunk(e, j), fwd_ss.at[n, j], fwd_rs.at[n, j], to, q)

        def across(e, t):
            send(g.at[e], g.at[e], core_ss.at[n, t], core_rs.at[n, t], other, q)

        for s in range(1, NZ):
            there = lax.rem(z + s, NZ)
            remote(zb.at[there], zb.at[there], z_ss.at[n, s], z_rs.at[n, there], d, x * NZ + there).wait_recv()

        for s in (2, 1, 3, 0):
            if s < NX:
                to = lax.rem(x + s, NX)
                for t in range(GROUP):
                    piece = zb[t // CAP, sel[to * GROUP + t]]
                    if s:
                        staged[n, s - 1, t] = piece
                    else:
                        g[d, x * GROUP + t] = piece
                if s:
                    here = g.at[d, pl.ds(x * GROUP, GROUP)]
                    send(staged.at[n, s - 1], here, x_ss.at[n, s - 1], x_rs.at[n, s - 1], d, to * NZ + z)
        spread(0)
        spread(1)
        waiting = [0, 1]
        for j, s in enumerate([t for t in (1, 3, 2) if t < NX], 2):
            from_x = lax.rem(x + s, NX)
            remote(
                staged.at[n, NX - s - 1], chunk(d, j), x_ss.at[n, NX - s - 1], x_rs.at[n, NX - s - 1], d, from_x * NZ + z
            ).wait_recv()
            spread(j)
            for w in waiting:
                forward(w)
            waiting = [j]
        across(d, 0)
        for w in waiting:
            forward(w)
        across(up, 1)
        across(down, 2)
        for j in range(len(chunks)):
            frm = down if j in to_up else up
            remote(chunk(far, j), chunk(far, j), fwd_ss.at[n, j], fwd_rs.at[n, j], frm, q).wait_recv()
        across(far, 3)
        for t, s in enumerate((0, 1, NY - 1, 2)):
            e = lax.rem(y + s, NY) * 2 + 1 - k
            remote(g.at[e], g.at[e], core_ss.at[n, t], core_rs.at[n, t], other, q).wait_recv()

        if n == 0:
            loads[3].wait()
        first_product(n)
        if n < STEPS - 1:
            pass_out[n + 1] = acc[0].astype(BF16)

    pltpu.make_async_copy(acc.at[0], fut_hbm.at[0], out_sem.at[STEPS]).start()
    second_product(STEPS - 1)
    pltpu.make_async_copy(acc.at[1], fut_hbm.at[1], out_sem.at[STEPS + 1]).start()
    for copy in sent:
        copy.wait_send()

    @pl.when(d == 0)
    def _():
        for n in range(STEPS):
            for e in range(1, PIECES):
                scatter(n, e).wait_send()

    @pl.when(d > 0)
    def _():
        for n in range(STEPS):
            passing(n).wait_send()

    for n in range(STEPS):
        pltpu.make_async_copy(outv.at[n], cur_hbm.at[n], out_sem.at[n]).wait()
    for h in range(2):
        pltpu.make_async_copy(acc.at[h], fut_hbm.at[h], out_sem.at[STEPS + h]).wait()


def local(incident, history, couplings, block_inverse, load_coeff, pattern, wanted):
    size = block_inverse.shape[1]
    mine = BLK * size
    q = lax.axis_index("row")
    x, z = q // NZ, q % NZ
    table = wanted.reshape(NX, NZ, NX, NZ, CAP)
    table = lax.dynamic_slice(table, (0, z, x, 0, 0), (NX, 1, 1, NZ, CAP))
    table = jnp.maximum(table, 0).reshape(NX * GROUP)
    anywhere = pl.BlockSpec(memory_space=pl.ANY)
    dma = pltpu.SemaphoreType.DMA
    currents, future = pl.pallas_call(
        kernel,
        out_shape=(
            jax.ShapeDtypeStruct((STEPS, BLK, PIECES, 16, size), BF16),
            jax.ShapeDtypeStruct((2, mine, size), F32),
        ),
        in_specs=[anywhere] * 4
        + [pl.BlockSpec(memory_space=pltpu.VMEM), pl.BlockSpec(memory_space=pltpu.SMEM), pl.BlockSpec(memory_space=pltpu.SMEM)],
        out_specs=(anywhere, anywhere),
        scratch_shapes=[
            pltpu.VMEM((STEPS, mine, size), BF16),
            pltpu.VMEM((2, mine, size), F32),
            pltpu.VMEM((2, mine, PICKS * size), BF16),
            pltpu.VMEM((BLK, size, size), F32),
            pltpu.VMEM((STEPS, BLK, PIECES, 16, size), BF16),
            pltpu.VMEM((STEPS, mine, size), BF16),
            pltpu.VMEM((STEPS, mine, size), BF16),
            pltpu.VMEM((STEPS, PIECES, BLK, 16, size), BF16),
            pltpu.VMEM((STEPS, NX - 1, GROUP, 16, size), BF16),
            *[pltpu.VMEM((NZ, BLK, 16, size), BF16) for _ in range(STEPS)],
            *[pltpu.VMEM((PIECES, SLOTS + BLK, 16, size), BF16) for _ in range(STEPS)],
            dma((4,)),
            dma((STEPS + 2,)),
            dma((STEPS,)), dma((STEPS,)),
            dma((STEPS, PIECES)), dma((STEPS,)),
            dma((STEPS, NZ)), dma((STEPS, NZ)),
            dma((STEPS, NX - 1)), dma((STEPS, NX - 1)),
            dma((STEPS, NX + 1)), dma((STEPS, NX + 1)),
            dma((STEPS, NX + 1)), dma((STEPS, NX + 1)),
            dma((STEPS, NX + 1)), dma((STEPS, NX + 1)),
            dma((STEPS, 4)), dma((STEPS, 4)),
        ],
        compiler_params=pltpu.CompilerParams(
            collective_id=0, has_side_effects=True, vmem_limit_bytes=40 * 2**20
        ),
        name="march",
    )(
        incident, history, couplings, block_inverse, load_coeff.reshape(BLK, size),
        pattern.reshape(-1), table,
    )
    return currents.reshape(STEPS, mine, size), future


def solution(mesh):
    in_specs = (
        P(None, "row", None),
        P("delay", "row", None),
        P("delay", "row", None),
        P("row", None, None),
        P("row"),
        P("delay", "row", None),
        P(),
    )
    out_specs = (P(None, "row", None), P("delay", "row", None))
    return jax.shard_map(local, mesh=mesh, in_specs=in_specs, out_specs=out_specs, check_vma=False)
```

time: 494 us -> 104 us (0.21)
  waiting for transfers between devices: 420 us -> 0 us
  Pallas kernels: 0 us -> 93.3 us
  matrix products: 15.3 us -> 0 us
  starting transfers between devices: 14.3 us -> 0 us
  between operations: 14.3 us -> 0.7 us
  local copies, waits for them, and re-layouts: 19.3 us -> 9.27 us
  other arithmetic: 7.82 us -> 0.01 us
    all_gather x3 -> x0, waiting for transfers between devices: 227 us -> none  [local(): source = lax.all_gather(blocks, 'row', axis=0, tiled=True)]
    psum x3 -> x0, waiting for transfers between devices: 192 us -> none  [spread(): return lax.psum(kept, axis)]
    pallas_call x0 -> x1, Pallas kernels: none -> 93.3 us  [local(): pl.pallas_call(kernel, out_shape=(jax.ShapeDtypeStruct((STEPS, BLK, PIECE...]
    gather x4 -> x0, local copies, waits for them, and re-layouts: 17.3 us -> none  [the longest x3 15.8 us: local(): source[position].reshape(local_delays, blk_rows, nonzero * size_blk, excite)]
    dot_general x6 -> x0, matrix products: 15.3 us -> none  [the longest x3 14.2 us: local(): jnp.einsum('krab,krbc->krac', zmats, picked, preferred_element_type=jnp.f...]
    ppermute x3 -> x0, starting transfers between devices: 14 us -> none  [passed_along(): lax.ppermute(value, axis, [(source, source + steps) for source in range(l...]
    unnamed x12 -> x13, local copies, waits for them, and re-layouts: 0.03 us -> 7.49 us
  transfers between devices with their start and end apart: 9 -> 0, of which waited for: 7 -> 0; matrix products, arithmetic and copies ran while one was open for 1% -> 0% of each run, Pallas kernels for 0% -> 0%
where the time goes in v1:
time: 104 us; the launch traced here: 103 us
  Pallas kernels  93.3 us (90%)
  local copies, waits for them, and re-layouts  9.27 us (9%)
    pallas_call x1, Pallas kernels, local(): pl.pallas_call(kernel, out_shape=(jax.ShapeDtypeStruct((STEPS, BLK, PIECE...  93.3 us
    unnamed x13, local copies, waits for them, and re-layouts  7.49 us

profile of v1, /device:TPU:1, one launch (start us, length us, event | category | flops | bytes accessed | tf_op | source)
XLA Modules:
  0.0 103.3 jit_solution(8837287034657795878)
XLA Ops:
  0.7 0.8 reshape.20.pat
  1.4 0.9 reshape.21
  2.4 0.1 copy.11
  2.5 0.1 reshape.22.sel
  2.6 0.0 copy-start
  2.6 2.2 %copy-done = bf16[2,512,2048]{2,1,0:T(8,128)(2,1)S(1)} copy-done((bf16[2,512,2048]{2,1,0:T(8,128)(2,1)S(1)}, bf16[2,512,2048]{2,1,0:T(8,128)(2,1)}, u32[]{:S(2)}) %copy-start) | copy-done | bytes 4194328
  4.8 0.0 copy-start.1
  4.8 1.0 %copy-done.1 = f32[2,512,128]{2,1,0:T(8,128)S(1)} copy-done((f32[2,512,128]{2,1,0:T(8,128)S(1)}, f32[2,512,128]{2,1,0:T(8,128)}, u32[]{:S(2)}) %copy-start.1) | copy-done | bytes 524312
  5.8 0.0 copy-start.2
  5.8 1.0 copy-done.2
  6.8 0.0 copy-start.3
  6.8 0.9 copy-done.3
  7.7 0.0 copy-start.4
  7.8 0.7 copy-done.4
  8.4 93.3 %march.1 = (bf16[3,4,8,16,128]{4,3,2,1,0:T(8,128)(2,1)S(1)}, f32[2,512,128]{2,1,0:T(8,128)S(1)}) custom-call(bf16[3,512,128]{2,1,0:T(8,128)(2,1)S(1)} %copy-done.2, f32[2,512,128]{2,1,0:T(8,128)S(1)} %copy-done.1, bf16[2,512,2048]{2,1,0:T(8,128)(2,1)S(1)} %copy-done, f32[4,128,128]{2,1,0:T(8,128)S(1)} %copy-done.3, f32[4,128]{1,0:T(4,128)S(1)} %bitcast.9, ...), custom_call_target="tpu_custom_call" | custom-call | tf_op jit(solution)/shard_map/march/pallas_call | solution.py:246
  101.7 0.7 copy.14
  102.5 0.8 copy.15
  (2 shorter events, 0.0 us)
Async XLA Ops:
  2.6 2.2 %copy-start = (bf16[2,512,2048]{2,1,0:T(8,128)(2,1)S(1)}, bf16[2,512,2048]{2,1,0:T(8,128)(2,1)}, u32[]{:S(2)}) copy-start(bf16[2,512,2048]{2,1,0:T(8,128)(2,1)} %z_hbm.1) | copy-start | bytes 12582916
  4.8 1.0 %copy-start.1 = (f32[2,512,128]{2,1,0:T(8,128)S(1)}, f32[2,512,128]{2,1,0:T(8,128)}, u32[]{:S(2)}) copy-start(f32[2,512,128]{2,1,0:T(8,128)} %hist_hbm.1) | copy-start | bytes 1572868
  5.8 1.0 copy-start.2
  6.8 0.9 copy-start.3
  7.7 0.7 copy-start.4

commit v2 on v1

v2 whole, which is shorter than its diff:
```python
import jax
import jax.numpy as jnp
from jax import lax
from jax.experimental import pallas as pl
from jax.experimental.pallas import tpu as pltpu
from jax.sharding import PartitionSpec as P

STEPS = 3
NX, NY, NZ = 4, 4, 8
PIECES = 2 * NY
BLK = 4
CAP = 2
GROUP = NZ * CAP
SLOTS = NX * GROUP
PICKS = 16
HELD = 3
TOGETHER = 4
BF16, F32 = jnp.bfloat16, jnp.float32
HIGHEST = lax.Precision.HIGHEST


def kernel(
    inc_hbm, hist_hbm, z_hbm, binv_hbm, pat_hbm, lc_ref, pat, wanted, cur_ref, fut_ref,
    inc, acc, zmat, binv, pass_out, pass_in, staged, cut, slices, share_z, pat_in, pat0, base, share, share_out, share_in, *rest,
):
    zblk, own, got = rest[:STEPS], rest[STEPS : 2 * STEPS], rest[2 * STEPS : 3 * STEPS]
    (
        local_sem, pass_ss, pass_rs, cut_ss, cut_rs, z_ss, z_rs, x_ss, x_rs, up_ss, up_rs, down_ss, down_rs,
        fwd_ss, fwd_rs, core_ss, core_rs, slice_ss, slice_rs, pat_ss, pat_rs, base_ss, base_rs, share_ss, share_rs,
    ) = rest[3 * STEPS :]
    d, q = lax.axis_index("delay"), lax.axis_index("row")
    y, k = d // 2, d % 2
    x, z = q // NZ, q % NZ
    rows = PIECES * 16
    up, down, far = (lax.rem(y + s, NY) * 2 + k for s in (1, NY - 1, 2))
    other = y * 2 + 1 - k
    sent = []

    def remote(src, dst, ss, rs, dd, qq):
        return pltpu.make_async_remote_copy(
            src_ref=src, dst_ref=dst, send_sem=ss, recv_sem=rs, device_id=(dd, qq),
            device_id_type=pl.DeviceIdType.MESH,
        )

    def send(*args):
        copy = remote(*args)
        copy.start()
        sent.append((copy, None))

    def send_if(cond, *args):
        copy = remote(*args)
        pl.when(cond)(copy.start)
        sent.append((copy, cond))

    loads = [
        pltpu.make_async_copy(hist_hbm, acc, local_sem.at[0]),
        pltpu.make_async_copy(inc_hbm, inc, local_sem.at[1]),
        pltpu.make_async_copy(binv_hbm, binv, local_sem.at[2]),
        pltpu.make_async_copy(z_hbm, zmat, local_sem.at[3]),
    ]
    for load in loads:
        load.start()

    barrier = pltpu.get_barrier_semaphore()
    peers = [(lax.rem(d + s, PIECES), q) for s in range(1, PIECES)]
    peers += [(d, x * NZ + lax.rem(z + s, NZ)) for s in range(1, NZ)]
    peers += [(d, lax.rem(x + s, NX) * NZ + z) for s in range(1, NX)]
    for peer in peers:
        pl.semaphore_signal(barrier, inc=1, device_id=peer, device_id_type=pl.DeviceIdType.MESH)

    def finish(b, rhs):
        load = jnp.broadcast_to(lc_ref[pl.ds(b, 1), :], (rows, rows)).T
        solved = jnp.dot(binv[b], rhs, precision=HIGHEST, preferred_element_type=F32)
        return (solved - load * solved * solved * solved).astype(BF16).reshape(PIECES, 16, rows)

    def part_of(b):
        return pl.ds(b * rows if isinstance(b, int) else pl.multiple_of(b * rows, rows), rows)

    def slice_z():
        def body(i, carry):
            for s in range(PICKS):
                tile = zmat[0, part_of(i), pl.ds(s * rows, rows)]
                slices[:, i, s] = tile.T.reshape(PIECES, 16, rows)
            return carry

        lax.fori_loop(0, BLK, body, 0)

    for load in loads[:3]:
        load.wait()

    @pl.when(d == 0)
    def _():
        for i in range(BLK):
            cut[0, :, i] = finish(i, inc[0, part_of(i), :].astype(F32) - acc[0, part_of(i), :])
        loads[3].wait()
        slice_z()
        share_z[...] = slices[0]
        base[0] = acc[1, part_of(0), :]

    @pl.when(d > 0)
    def _():
        loads[3].wait()

    pass_out[0] = acc[0].astype(BF16)

    @pl.when(d == PIECES - 1)
    def _():
        pass_in[...] = jnp.zeros_like(pass_in)

    pl.semaphore_wait(barrier, len(peers))

    def passing(n):
        return remote(pass_out.at[n], pass_in.at[n], pass_ss.at[n], pass_rs.at[n], lax.rem(d + PIECES - 1, PIECES), q)

    def pass_on(n):
        pl.when(d > 0)(passing(n).start)
        sent.append((passing(n), d > 0))

    def product(n, half, i):
        total = None
        for s in range(0, PICKS, TOGETHER):
            picked = [got[n][:, pat[half, i, s + t]].reshape(rows, rows) for t in range(TOGETHER)]
            part = jnp.dot(
                zmat[half, part_of(i), pl.ds(s * rows, TOGETHER * rows)],
                jnp.concatenate(picked, axis=0),
                preferred_element_type=F32,
            )
            total = part if total is None else total + part
        return total

    def first_product(n, out):
        def body(i, carry):
            out[0, part_of(i), :] = acc[1, part_of(i), :] + product(n, 0, i)
            return carry

        lax.fori_loop(0, BLK, body, 0)

    def second_product(n, out):
        @pl.when(d < PIECES - 1)
        def _():
            passing(n).wait_recv()

        def body(i, carry):
            out[1, part_of(i), :] = pass_in[n, part_of(i), :].astype(F32) + product(n, 1, i)
            return carry

        lax.fori_loop(0, BLK, body, 0)
        cur_ref[n] = got[n][:, pl.ds(SLOTS, BLK)].transpose(1, 0, 2, 3)

    def products(n):
        @pl.when(d > 0)
        def _():
            first_product(n, acc)
            pass_out[n + 1] = acc[0].astype(BF16)

        pass_on(n + 1)
        if n == 1:
            @pl.when(d == 0)
            def _():
                for b in range(1, BLK):
                    remote(*base_args(1, b)).wait_send()

        second_product(n, acc)
        if n == 0:
            @pl.when(d == 0)
            def _():
                for b in range(1, BLK):
                    remote(*base_args(1, b)).start()
                base[1] = acc[1, part_of(0), :]

    def base_args(m, b):
        src = hist_hbm.at[1, part_of(b)] if m == 0 else acc.at[1, part_of(b)]
        return src, base.at[m], base_ss.at[m, b], base_rs.at[m], 2 * b, q

    xs = [s for s in (1, 3, 2) if s < NX]
    chunks = [(SLOTS, BLK)] + [(lax.rem(x + s, NX) * GROUP, GROUP) for s in (0, *xs)]
    to_up = [j for j in (1, 3) if j < len(chunks)]

    def chunk(n, e, j):
        return got[n].at[e, pl.ds(*chunks[j])]

    def spread(n, j):
        src = own[n].at[pl.ds(*chunks[j])]
        send(src, chunk(n, d, j), up_ss.at[n, j], up_rs.at[n, j], up, q)
        send(src, chunk(n, d, j), down_ss.at[n, j], down_rs.at[n, j], down, q)

    def forward(n, j):
        remote(chunk(n, down, j), chunk(n, down, j), up_ss.at[n, j], up_rs.at[n, j], down, q).wait_recv()
        remote(chunk(n, up, j), chunk(n, up, j), down_ss.at[n, j], down_rs.at[n, j], up, q).wait_recv()
        e, to = (down, up) if j in to_up else (up, down)
        send(chunk(n, e, j), chunk(n, e, j), fwd_ss.at[n, j], fwd_rs.at[n, j], to, q)

    def across(n, e, t):
        src = own[n] if t == 0 else got[n].at[e]
        send(src, got[n].at[e], core_ss.at[n, t], core_rs.at[n, t], other, q)

    def forwards(n, js):
        for j in js:
            forward(n, j)

    def last_hops(n):
        for j in range(len(chunks)):
            frm = down if j in to_up else up
            remote(chunk(n, far, j), chunk(n, far, j), fwd_ss.at[n, j], fwd_rs.at[n, j], frm, q).wait_recv()
        across(n, far, 3)

    def gathered(n):
        for t, s in enumerate((0, 1, NY - 1, 2)):
            e = lax.rem(y + s, NY) * 2 + 1 - k
            remote(got[n].at[e], got[n].at[e], core_ss.at[n, t], core_rs.at[n, t], other, q).wait_recv()

    for n in range(STEPS):
        zb = zblk[n]
        if n == 0:
            for e in range(1, PIECES):
                send_if(d == 0, cut.at[0, e], zb.at[z], cut_ss.at[0, e], cut_rs.at[0, 0], e, q)

            @pl.when(d == 0)
            def _():
                zb[z] = cut[0, 0]

            @pl.when(d > 0)
            def _():
                remote(cut.at[0, 1], zb.at[z], cut_ss.at[0, 1], cut_rs.at[0, 0], 0, q).wait_recv()

        else:
            m = n - 1

            @pl.when(k == 0)
            def _():
                @pl.when(d > 0)
                def _():
                    remote(base.at[m], base.at[m], base_ss.at[m, 1], base_rs.at[m], 0, q).wait_recv()

                rhs = inc[n, part_of(y), :].astype(F32) - base[m] - share[y]
                for s in range(1, PIECES):
                    e = lax.rem(d + s, PIECES)
                    here = share_in.at[m, e]
                    remote(here, here, share_ss.at[m, 0], share_rs.at[m, e], e, q).wait_recv()
                    rhs = rhs - share_in[m, e].astype(F32)
                cut[n, :, 0] = finish(y, rhs)

            for s in range(1, PIECES):
                e = lax.rem(d + s, PIECES)
                send_if(k == 0, cut.at[n, e, 0], zb.at[z, y], cut_ss.at[n, s], cut_rs.at[n, y], e, q)

            @pl.when(k == 0)
            def _():
                zb[z, y] = cut[n, d, 0]

            for b in range(BLK):
                @pl.when(d != 2 * b)
                def _():
                    remote(zb.at[z, b], zb.at[z, b], cut_ss.at[n, 1], cut_rs.at[n, b], 2 * b, q).wait_recv()

        for s in (4, 3, 5, 2, 6, 1, 7):
            if s < NZ:
                to = lax.rem(z + s, NZ)
                send(zb.at[z], zb.at[z], z_ss.at[n, s], z_rs.at[n, z], d, x * NZ + to)
        own[n][pl.ds(SLOTS, BLK)] = zb[z]
        if n == 0:
            for e in range(1, PIECES):
                send_if(d == 0, pat_hbm, pat_in, pat_ss.at[e], pat_rs.at[0], e, q)
            for e in (4, 5, 2, 3, 6, 7, 1):
                send_if(d == 0, slices.at[e], share_z, slice_ss.at[e], slice_rs.at[0], e, q)
            for b in range(1, BLK):
                send_if(d == 0, *base_args(0, b))
            pass_on(0)
        else:
            for j in range(HELD, len(chunks)):
                spread(n - 1, j)

        for s in range(1, NZ):
            there = lax.rem(z + s, NZ)
            remote(zb.at[there], zb.at[there], z_ss.at[n, s], z_rs.at[n, there], d, x * NZ + there).wait_recv()

        for s in (2, 1, 3, 0):
            if s < NX:
                to = lax.rem(x + s, NX)
                for t in range(GROUP):
                    piece = zb[t // CAP, jnp.maximum(wanted[to * NZ + z, t % CAP, x * NZ + t // CAP], 0)]
                    if s:
                        staged[n, s - 1, t] = piece
                    else:
                        own[n][x * GROUP + t] = piece
                if s:
                    here = own[n].at[pl.ds(x * GROUP, GROUP)]
                    send(staged.at[n, s - 1], here, x_ss.at[n, s - 1], x_rs.at[n, s - 1], d, to * NZ + z)

        if n == 0:
            @pl.when(d > 0)
            def _():
                remote(pat_hbm, pat_in, pat_ss.at[1], pat_rs.at[0], 0, q).wait_recv()

            @pl.when(d == 0)
            def _():
                copy = pltpu.make_async_copy(pat_hbm, pat_in, local_sem.at[4])
                copy.start()
                copy.wait()

            copy = pltpu.make_async_copy(pat_in, pat0, local_sem.at[5])
            copy.start()
            copy.wait()
        else:
            forwards(n - 1, range(len(chunks)))
            across(n - 1, up, 1)
            across(n - 1, down, 2)
            last_hops(n - 1)
        if n == STEPS - 1:
            spread(n, 0)
            spread(n, 1)

        for j, s in enumerate(xs, 2):
            from_x = lax.rem(x + s, NX)
            there = own[n].at[pl.ds(*chunks[j])]
            back = NX - s - 1
            remote(staged.at[n, back], there, x_ss.at[n, back], x_rs.at[n, back], d, from_x * NZ + z).wait_recv()
            if n == STEPS - 1:
                spread(n, j)
        if n == STEPS - 1:
            across(n, d, 0)
        got[n][d] = own[n][...]

        if n < STEPS - 1:
            if n == 0:
                @pl.when(d > 0)
                def _():
                    remote(share_z, share_z, slice_ss.at[1], slice_rs.at[0], 0, q).wait_recv()

            def body(i, carry):
                picked = jnp.concatenate([own[n][pat0[0, i, s]] for s in range(PICKS)], axis=0)
                total = lax.dot_general(
                    share_z[i].reshape(PICKS * 16, rows), picked, (((0,), (0,)), ((), ())), preferred_element_type=F32
                )
                share[i] = total
                share_out[n, i] = total.astype(BF16)
                return carry

            lax.fori_loop(0, BLK, body, 0)
            for b in range(BLK):
                send_if(d != 2 * b, share_out.at[n, b], share_in.at[n, d], share_ss.at[n, b], share_rs.at[n, d], 2 * b, q)
            for j in range(HELD):
                spread(n, j)
            across(n, d, 0)
        if n:
            gathered(n - 1)
            products(n - 1)

    n = STEPS - 1
    forwards(n, range(len(chunks)))
    across(n, up, 1)
    across(n, down, 2)
    last_hops(n)
    gathered(n)
    first_product(n, fut_ref)
    second_product(n, fut_ref)
    for copy, cond in sent:
        if cond is None:
            copy.wait_send()
        else:
            pl.when(cond)(copy.wait_send)


def local(incident, history, couplings, block_inverse, load_coeff, pattern, wanted):
    size = block_inverse.shape[1]
    mine = BLK * size
    anywhere = pl.BlockSpec(memory_space=pl.ANY)
    numbers = pl.BlockSpec(memory_space=pltpu.SMEM)
    dma = pltpu.SemaphoreType.DMA
    chunk_sems = [dma((STEPS, NX + 1)) for _ in range(6)]
    currents, future = pl.pallas_call(
        kernel,
        out_shape=(
            pltpu.VMEM((STEPS, BLK, PIECES, 16, size), BF16),
            pltpu.VMEM((2, mine, size), F32),
        ),
        in_specs=[anywhere] * 5 + [pl.BlockSpec(memory_space=pltpu.VMEM), numbers, numbers],
        out_specs=(pl.BlockSpec(memory_space=pltpu.VMEM), pl.BlockSpec(memory_space=pltpu.VMEM)),
        scratch_shapes=[
            pltpu.VMEM((STEPS, mine, size), BF16),
            pltpu.VMEM((2, mine, size), F32),
            pltpu.VMEM((2, mine, PICKS * size), BF16),
            pltpu.VMEM((BLK, size, size), F32),
            pltpu.VMEM((STEPS, mine, size), BF16),
            pltpu.VMEM((STEPS, mine, size), BF16),
            pltpu.VMEM((STEPS, NX - 1, GROUP, 16, size), BF16),
            pltpu.VMEM((STEPS, PIECES, BLK, 16, size), BF16),
            pltpu.VMEM((PIECES, BLK, PICKS, 16, size), BF16),
            pltpu.VMEM((BLK, PICKS, 16, size), BF16),
            pltpu.VMEM(pattern.shape, jnp.int32),
            pltpu.SMEM(pattern.shape, jnp.int32),
            pltpu.VMEM((STEPS - 1, size, size), F32),
            pltpu.VMEM((BLK, size, size), F32),
            pltpu.VMEM((STEPS - 1, BLK, size, size), BF16),
            pltpu.VMEM((STEPS - 1, PIECES, size, size), BF16),
            *[pltpu.VMEM((NZ, BLK, 16, size), BF16) for _ in range(STEPS)],
            *[pltpu.VMEM((SLOTS + BLK, 16, size), BF16) for _ in range(STEPS)],
            *[pltpu.VMEM((PIECES, SLOTS + BLK, 16, size), BF16) for _ in range(STEPS)],
            dma((6,)),
            dma((STEPS,)), dma((STEPS,)),
            dma((STEPS, PIECES)), dma((STEPS, BLK)),
            dma((STEPS, NZ)), dma((STEPS, NZ)),
            dma((STEPS, NX - 1)), dma((STEPS, NX - 1)),
            *chunk_sems,
            dma((STEPS, 4)), dma((STEPS, 4)),
            dma((PIECES,)), dma((1,)),
            dma((PIECES,)), dma((1,)),
            dma((STEPS - 1, BLK)), dma((STEPS - 1,)),
            dma((STEPS - 1, BLK)), dma((STEPS - 1, PIECES)),
        ],
        compiler_params=pltpu.CompilerParams(
            collective_id=0, has_side_effects=True, vmem_limit_bytes=60 * 2**20
        ),
        name="march",
    )(
        incident, history, couplings, block_inverse, pattern, load_coeff.reshape(BLK, size),
        pattern, wanted.transpose(0, 2, 1),
    )
    return currents.reshape(STEPS, mine, size), future


def solution(mesh):
    in_specs = (
        P(None, "row", None),
        P("delay", "row", None),
        P("delay", "row", None),
        P("row", None, None),
        P("row"),
        P("delay", "row", None),
        P(),
    )
    out_specs = (P(None, "row", None), P("delay", "row", None))
    return jax.shard_map(local, mesh=mesh, in_specs=in_specs, out_specs=out_specs, check_vma=False)
```

time: 104 us -> 87.1 us (0.84)
  Pallas kernels: 93.3 us -> 84.7 us
  local copies, waits for them, and re-layouts: 9.27 us -> 1.54 us
    pallas_call x1, Pallas kernels: 93.3 us -> 84.7 us  [local(): pl.pallas_call(kernel, out_shape=(pltpu.VMEM((STEPS, BLK, PIECES, 16, siz...]
    unnamed x13 -> x2, local copies, waits for them, and re-layouts: 7.49 us -> 1.54 us
    reshape x3 -> x0, local copies, waits for them, and re-layouts: 1.77 us -> none  [the longest x1 0.9 us: local(): table = wanted.reshape(NX, NZ, NX, NZ, CAP)]
where the time goes in v2:
time: 87.1 us; the launch traced here: 86.9 us
  Pallas kernels  84.7 us (97%)
  local copies, waits for them, and re-layouts  1.54 us (2%)
    pallas_call x1, Pallas kernels, local(): pl.pallas_call(kernel, out_shape=(pltpu.VMEM((STEPS, BLK, PIECES, 16, siz...  84.7 us

profile of v2, /device:TPU:1, one launch (start us, length us, event | category | flops | bytes accessed | tf_op | source)
XLA Modules:
  0.0 86.9 jit_solution(16183906976178033454)
XLA Ops:
  0.6 84.7 %march.1 = (bf16[3,4,8,16,128]{4,3,2,1,0:T(8,128)(2,1)S(1)}, f32[2,512,128]{2,1,0:T(8,128)S(1)}) custom-call(bf16[3,512,128]{2,1,0:T(8,128)(2,1)} %inc_hbm.1, f32[2,512,128]{2,1,0:T(8,128)} %hist_hbm.1, bf16[2,512,2048]{2,1,0:T(8,128)(2,1)} %z_hbm.1, f32[4,128,128]{2,1,0:T(8,128)} %binv_hbm.1, s32[2,4,16]{2,1,0:T(4,128)} %pat.1, f32[4,128]{1,0:T(4,128)} %bitcast.5, ...), custom_call_target="tpu_custom_call" | custom-call | tf_op jit(solution)/shard_map/march/pallas_call | solution.py:371
  85.3 0.7 copy.11
  86.1 0.8 copy.12

commit v3 on v0

v3 whole, which is shorter than its diff:
```python
import jax
import jax.numpy as jnp
from jax import lax
from jax.experimental import pallas as pl
from jax.experimental.pallas import tpu as pltpu
from jax.sharding import PartitionSpec as P

STEPS = 3
NX, NY, NZ = 4, 4, 8
OWNERS = NX * NZ
PIECES = 2 * NY
BLK = 4
CAP = 2
GROUP = NZ * CAP
SLOTS = NX * GROUP
PICKS = 16
TOGETHER = 4
EARLY = (1, 2, 6)
BF16, F32 = jnp.bfloat16, jnp.float32
HIGHEST = lax.Precision.HIGHEST


def kernel(
    inc_hbm, hist_hbm, z_hbm, binv_hbm, pat_hbm, lc_ref, pat, wanted, cur_ref, fut_ref,
    inc, acc, zmat, binv, load, pass_out, pass_in, staged, cut, slices, share_z, pat_in, pat0,
    base_out, base, share, share_out, share_in, *rest,
):
    mine, own, got = rest[:STEPS], rest[STEPS : 2 * STEPS], rest[2 * STEPS : 3 * STEPS]
    (
        local_sem, pass_ss, pass_rs, cut_ss, cut_rs, plane_ss, plane_rs, y_ss, y_rs, core_ss, core_rs,
        slice_ss, slice_rs, pat_ss, pat_rs, base_ss, base_rs, share_ss, share_rs,
    ) = rest[3 * STEPS :]
    d, q = lax.axis_index("delay"), lax.axis_index("row")
    y, k = d // 2, d % 2
    x, z = q // NZ, q % NZ
    rows = PIECES * 16
    other = y * 2 + 1 - k
    sent = []

    def remote(src, dst, ss, rs, dd, qq):
        return pltpu.make_async_remote_copy(
            src_ref=src, dst_ref=dst, send_sem=ss, recv_sem=rs, device_id=(dd, qq),
            device_id_type=pl.DeviceIdType.MESH,
        )

    def send(*args):
        copy = remote(*args)
        copy.start()
        sent.append((copy, None))

    def send_if(cond, *args):
        copy = remote(*args)
        pl.when(cond)(copy.start)
        sent.append((copy, cond))

    def arrived(dst, rs):
        remote(dst, dst, rs, rs, other, q).wait_recv()

    def left(src, ss):
        remote(src, src, ss, ss, other, q).wait_send()

    loads = [
        pltpu.make_async_copy(hist_hbm, acc, local_sem.at[0]),
        pltpu.make_async_copy(inc_hbm, inc, local_sem.at[1]),
        pltpu.make_async_copy(binv_hbm, binv, local_sem.at[2]),
        pltpu.make_async_copy(z_hbm, zmat, local_sem.at[3]),
    ]
    for start in loads:
        start.start()

    around = [lax.rem(d + s, PIECES) for s in range(1, PIECES)]
    plane = [
        lax.rem(x + a, NX) * NZ + lax.rem(z + s, NZ) for a in (0, 1, 3, 2) for s in (4, 3, 5, 2, 6, 1, 7, 0) if a or s
    ]
    barrier = pltpu.get_barrier_semaphore()
    peers = [(e, q) for e in around] + [(d, p) for p in plane]
    for peer in peers:
        pl.semaphore_signal(barrier, inc=1, device_id=peer, device_id_type=pl.DeviceIdType.MESH)

    def part_of(b):
        return pl.ds(b * rows if isinstance(b, int) else pl.multiple_of(b * rows, rows), rows)

    def invert(b, rhs):
        solved = jnp.dot(binv[b], rhs, precision=HIGHEST, preferred_element_type=F32)
        return solved.reshape(PIECES, 16, rows)

    def loaded(solved, coefficient):
        return (solved - coefficient * solved * solved * solved).astype(BF16)

    def slice_z(half):
        def body(i, carry):
            for s in range(PICKS):
                tile = zmat[half, part_of(i), pl.ds(s * rows, rows)]
                slices[half, :, i, s] = tile.T.reshape(PIECES, 16, rows)
            return carry

        lax.fori_loop(0, BLK, body, 0)

    for start in loads[:3]:
        start.wait()
    for i in range(BLK):
        load[i] = jnp.broadcast_to(lc_ref[pl.ds(i, 1), :], (rows, rows)).T.reshape(PIECES, 16, rows)

    @pl.when(d == 0)
    def _():
        for i in range(BLK):
            cut[:, i] = loaded(invert(i, inc[0, part_of(i), :].astype(F32) - acc[0, part_of(i), :]), load[i])
        mine[0][...] = cut[0]

    loads[3].wait()

    @pl.when(d == 0)
    def _():
        slice_z(0)
        share_z[0] = slices[0, 0]

    @pl.when(d < 2)
    def _():
        for i in range(BLK):
            base_out[:, i] = invert(i, inc[1 + d, part_of(i), :].astype(F32) - acc[1 - d, part_of(i), :])
        base[d] = base_out[d]

    pass_out[0] = acc[0].astype(BF16)

    @pl.when(d == PIECES - 1)
    def _():
        pass_in[...] = jnp.zeros_like(pass_in)

    pl.semaphore_wait(barrier, len(peers))

    def passing(n):
        return remote(pass_out.at[n], pass_in.at[n], pass_ss.at[n], pass_rs.at[n], lax.rem(d + PIECES - 1, PIECES), q)

    def pass_on(n):
        pl.when(d > 0)(passing(n).start)
        sent.append((passing(n), d > 0))

    def send_slices(half, which):
        for e in which:
            send_if(d == 0, slices.at[half, e], share_z.at[half], slice_ss.at[half, e], slice_rs.at[half], e, q)

    def product(n, half, i):
        total = None
        for s in range(0, PICKS, TOGETHER):
            picked = [got[n][:, pat[half, i, s + t]].reshape(rows, rows) for t in range(TOGETHER)]
            part = jnp.dot(
                zmat[half, part_of(i), pl.ds(s * rows, TOGETHER * rows)],
                jnp.concatenate(picked, axis=0),
                preferred_element_type=F32,
            )
            total = part if total is None else total + part
        return total

    def products(n, out):
        def first(i, carry):
            out[0, part_of(i), :] = acc[1, part_of(i), :] + product(n, 0, i)
            return carry

        lax.fori_loop(0, BLK, first, 0)
        if n < STEPS - 1:
            pass_out[n + 1] = out[0].astype(BF16)
            pass_on(n + 1)

        @pl.when(d < PIECES - 1)
        def _():
            arrived(pass_in.at[n], pass_rs.at[n])

        def second(i, carry):
            out[1, part_of(i), :] = pass_in[n, part_of(i), :].astype(F32) + product(n, 1, i)
            return carry

        lax.fori_loop(0, BLK, second, 0)
        cur_ref[n] = got[n][:, pl.ds(SLOTS, BLK)].transpose(1, 0, 2, 3)

    chunks = [(SLOTS, BLK)] + [(lax.rem(x + a, NX) * GROUP, GROUP) for a in (0, 3, 1, 2)]

    def spread(n, j):
        here = pl.ds(*chunks[j])
        for t, s in enumerate((2, 1, 3)):
            remote(
                own[n].at[here], got[n].at[d, here], y_ss.at[n, t], y_rs.at[n, t], lax.rem(y + s, NY) * 2 + k, q
            ).start()

    def across(n, e, t):
        src = own[n] if t == 3 else got[n].at[e]
        send(src, got[n].at[e], core_ss.at[n, t], core_rs.at[n, t], other, q)

    def hand_over(n):
        for t, s in enumerate((2, 1, 3)):
            e = lax.rem(y + NY - s, NY) * 2 + k
            arrived(got[n].at[e], y_rs.at[n, t])
            across(n, e, t)

    def gathered(n):
        for t, s in enumerate((2, 1, 3, 0)):
            arrived(got[n].at[lax.rem(y + NY - s, NY) * 2 + 1 - k], core_rs.at[n, t])

    for n in range(STEPS):
        if n == 0:
            for e in range(1, PIECES):
                send_if(d == 0, cut.at[e], mine[0], cut_ss.at[e], cut_rs.at[0], e, q)
            for e in range(1, PIECES):
                send_if(d == 0, pat_hbm, pat_in, pat_ss.at[e], pat_rs.at[0], e, q)
            send_slices(0, (4, 5, 2, 3, 6, 7, 1))

            @pl.when(d > 0)
            def _():
                arrived(mine[0], cut_rs.at[0])

        else:
            m = n - 1

            @pl.when(d != m)
            def _():
                arrived(base.at[m], base_rs.at[m])

            arrived(share_in.at[m, pl.ds(0, PIECES - 1)], share_rs.at[m])
            for i in range(BLK):
                solved = base[m, i] - share[i, d]
                for e in around:
                    solved = solved - share_in[m, e, i].astype(F32)
                mine[n][i] = loaded(solved, load[i, d])

        for t, p in enumerate(plane):
            for c in range(CAP):
                staged[n, t, c] = mine[n][jnp.maximum(wanted[p, c, q], 0)]
            remote(staged.at[n, t], own[n].at[pl.ds(q * CAP, CAP)], plane_ss.at[n], plane_rs.at[n, x], d, p).start()
        for c in range(CAP):
            own[n][q * CAP + c] = mine[n][jnp.maximum(wanted[q, c, q], 0)]
        own[n][pl.ds(SLOTS, BLK)] = mine[n][...]

        if n == 0:
            for m in range(2):
                for s, e in enumerate(around):
                    send_if(d == m, base_out.at[e], base.at[m], base_ss.at[m, s], base_rs.at[m], e, q)
            pass_on(0)

            @pl.when(d == 0)
            def _():
                slice_z(1)
                share_z[1] = slices[1, 0]

            send_slices(1, EARLY)

            @pl.when(d > 0)
            def _():
                arrived(pat_in, pat_rs.at[0])

            @pl.when(d == 0)
            def _():
                copy = pltpu.make_async_copy(pat_hbm, pat_in, local_sem.at[4])
                copy.start()
                copy.wait()

            copy = pltpu.make_async_copy(pat_in, pat0, local_sem.at[5])
            copy.start()
            copy.wait()
        if n == STEPS - 1:
            gathered(n - 2)
            products(n - 2, acc)
            spread(n, 0)

        for j, a in enumerate((0, 3, 1, 2), 1):
            from_x = lax.rem(x + a, NX)
            there = pl.ds(0, GROUP - CAP) if a == 0 else pl.ds(*chunks[j])
            arrived(own[n].at[there], plane_rs.at[n, from_x])
            if n == STEPS - 1:
                spread(n, j)
        got[n][d] = own[n][...]

        if n < STEPS - 1:
            @pl.when(d > 0)
            def _():
                arrived(share_z.at[n], slice_rs.at[n])

            def body(i, carry):
                total = None
                for half in range(n + 1):
                    picked = jnp.concatenate([own[n - half][pat0[half, i, s]] for s in range(PICKS)], axis=0)
                    part = lax.dot_general(
                        share_z[half, i].reshape(PICKS * 16, rows), picked, (((0,), (0,)), ((), ())),
                        preferred_element_type=F32,
                    )
                    total = part if total is None else total + part
                solved = invert(i, total)
                share[i] = solved
                share_out[n, :, i] = solved.astype(BF16)
                return carry

            lax.fori_loop(0, BLK, body, 0)
            for s, e in enumerate(around):
                send(share_out.at[n, e], share_in.at[n, d], share_ss.at[n, s], share_rs.at[n], e, q)
            if n == 0:
                send_slices(1, [e for e in (4, 5, 3, 7) if e not in EARLY])
            for j in range(len(chunks)):
                spread(n, j)
        across(n, d, 3)
        if n:
            hand_over(n - 1)

    gathered(n - 1)
    products(n - 1, acc)
    hand_over(n)
    gathered(n)
    products(n, fut_ref)
    for n in range(STEPS):
        left(staged.at[n], plane_ss.at[n])
        for t in range(NY - 1):
            left(own[n], y_ss.at[n, t])
    for copy, cond in sent:
        if cond is None:
            copy.wait_send()
        else:
            pl.when(cond)(copy.wait_send)


def local(incident, history, couplings, block_inverse, load_coeff, pattern, wanted):
    size = block_inverse.shape[1]
    rows = BLK * size
    anywhere = pl.BlockSpec(memory_space=pl.ANY)
    numbers = pl.BlockSpec(memory_space=pltpu.SMEM)
    vmem = pl.BlockSpec(memory_space=pltpu.VMEM)
    dma = pltpu.SemaphoreType.DMA
    currents, future = pl.pallas_call(
        kernel,
        out_shape=(
            pltpu.VMEM((STEPS, BLK, PIECES, 16, size), BF16),
            pltpu.VMEM((2, rows, size), F32),
        ),
        in_specs=[anywhere] * 5 + [vmem, numbers, numbers],
        out_specs=(vmem, vmem),
        scratch_shapes=[
            pltpu.VMEM((STEPS, rows, size), BF16),
            pltpu.VMEM((2, rows, size), F32),
            pltpu.VMEM((2, rows, PICKS * size), BF16),
            pltpu.VMEM((BLK, size, size), F32),
            pltpu.VMEM((BLK, PIECES, 16, size), F32),
            pltpu.VMEM((STEPS, rows, size), BF16),
            pltpu.VMEM((STEPS, rows, size), BF16),
            pltpu.VMEM((STEPS, OWNERS - 1, CAP, 16, size), BF16),
            pltpu.VMEM((PIECES, BLK, 16, size), BF16),
            pltpu.VMEM((2, PIECES, BLK, PICKS, 16, size), BF16),
            pltpu.VMEM((2, BLK, PICKS, 16, size), BF16),
            pltpu.VMEM(pattern.shape, jnp.int32),
            pltpu.SMEM(pattern.shape, jnp.int32),
            pltpu.VMEM((PIECES, BLK, 16, size), F32),
            pltpu.VMEM((STEPS - 1, BLK, 16, size), F32),
            pltpu.VMEM((BLK, PIECES, 16, size), F32),
            pltpu.VMEM((STEPS - 1, PIECES, BLK, 16, size), BF16),
            pltpu.VMEM((STEPS - 1, PIECES, BLK, 16, size), BF16),
            *[pltpu.VMEM((BLK, 16, size), BF16) for _ in range(STEPS)],
            *[pltpu.VMEM((SLOTS + BLK, 16, size), BF16) for _ in range(STEPS)],
            *[pltpu.VMEM((PIECES, SLOTS + BLK, 16, size), BF16) for _ in range(STEPS)],
            dma((6,)),
            dma((STEPS,)), dma((STEPS,)),
            dma((PIECES,)), dma((1,)),
            dma((STEPS,)), dma((STEPS, NX)),
            dma((STEPS, NY - 1)), dma((STEPS, NY - 1)),
            dma((STEPS, NY)), dma((STEPS, NY)),
            dma((2, PIECES)), dma((2,)),
            dma((PIECES,)), dma((1,)),
            dma((2, PIECES)), dma((2,)),
            dma((STEPS - 1, PIECES)), dma((STEPS - 1,)),
        ],
        compiler_params=pltpu.CompilerParams(
            collective_id=0, has_side_effects=True, vmem_limit_bytes=60 * 2**20
        ),
        name="march",
    )(
        incident, history, couplings, block_inverse, pattern, load_coeff.reshape(BLK, size),
        pattern, wanted.transpose(0, 2, 1),
    )
    return currents.reshape(STEPS, rows, size), future


def solution(mesh):
    in_specs = (
        P(None, "row", None),
        P("delay", "row", None),
        P("delay", "row", None),
        P("row", None, None),
        P("row"),
        P("delay", "row", None),
        P(),
    )
    out_specs = (P(None, "row", None), P("delay", "row", None))
    return jax.shard_map(local, mesh=mesh, in_specs=in_specs, out_specs=out_specs, check_vma=False)
```

time: 494 us -> 88.6 us (0.18)
  waiting for transfers between devices: 420 us -> 0 us
  Pallas kernels: 0 us -> 86.2 us
  local copies, waits for them, and re-layouts: 19.3 us -> 1.54 us
  matrix products: 15.3 us -> 0 us
  starting transfers between devices: 14.3 us -> 0 us
  between operations: 14.3 us -> 0.64 us
  other arithmetic: 7.82 us -> 0 us
    all_gather x3 -> x0, waiting for transfers between devices: 227 us -> none  [local(): source = lax.all_gather(blocks, 'row', axis=0, tiled=True)]
    psum x3 -> x0, waiting for transfers between devices: 192 us -> none  [spread(): return lax.psum(kept, axis)]
    pallas_call x0 -> x1, Pallas kernels: none -> 86.2 us  [local(): pl.pallas_call(kernel, out_shape=(pltpu.VMEM((STEPS, BLK, PIECES, 16, siz...]
    gather x4 -> x0, local copies, waits for them, and re-layouts: 17.3 us -> none  [the longest x3 15.8 us: local(): source[position].reshape(local_delays, blk_rows, nonzero * size_blk, excite)]
    dot_general x6 -> x0, matrix products: 15.3 us -> none  [the longest x3 14.2 us: local(): jnp.einsum('krab,krbc->krac', zmats, picked, preferred_element_type=jnp.f...]
    ppermute x3 -> x0, starting transfers between devices: 14 us -> none  [passed_along(): lax.ppermute(value, axis, [(source, source + steps) for source in range(l...]
  transfers between devices with their start and end apart: 9 -> 0, of which waited for: 7 -> 0; matrix products, arithmetic and copies ran while one was open for 1% -> 0% of each run, Pallas kernels for 0% -> 0%
where the time goes in v3:
time: 88.6 us; the launch traced here: 88.4 us
  Pallas kernels  86.2 us (97%)
  local copies, waits for them, and re-layouts  1.54 us (2%)
    pallas_call x1, Pallas kernels, local(): pl.pallas_call(kernel, out_shape=(pltpu.VMEM((STEPS, BLK, PIECES, 16, siz...  86.2 us

profile of v3, /device:TPU:1, one launch (start us, length us, event | category | flops | bytes accessed | tf_op | source)
XLA Modules:
  0.0 88.4 jit_solution(14290217118142432208)
XLA Ops:
  0.6 86.2 %march.1 = (bf16[3,4,8,16,128]{4,3,2,1,0:T(8,128)(2,1)S(1)}, f32[2,512,128]{2,1,0:T(8,128)S(1)}) custom-call(bf16[3,512,128]{2,1,0:T(8,128)(2,1)} %inc_hbm.1, f32[2,512,128]{2,1,0:T(8,128)} %hist_hbm.1, bf16[2,512,2048]{2,1,0:T(8,128)(2,1)} %z_hbm.1, f32[4,128,128]{2,1,0:T(8,128)} %binv_hbm.1, s32[2,4,16]{2,1,0:T(4,128)} %pat.1, f32[4,128]{1,0:T(4,128)} %bitcast.5, ...), custom_call_target="tpu_custom_call" | custom-call | tf_op jit(solution)/shard_map/march/pallas_call | solution.py:324
  86.8 0.7 copy.11
  87.6 0.8 copy.12

commit v4 on v3

--- a/solution.py
+++ b/solution.py
@@ -14,7 +14,7 @@
 GROUP = NZ * CAP
 SLOTS = NX * GROUP
 PICKS = 16
-TOGETHER = 4
+TOGETHER = 16
 EARLY = (1, 2, 6)
 BF16, F32 = jnp.bfloat16, jnp.float32
 HIGHEST = lax.Precision.HIGHEST
@@ -22,19 +22,20 @@
 
 def kernel(
     inc_hbm, hist_hbm, z_hbm, binv_hbm, pat_hbm, lc_ref, pat, wanted, cur_ref, fut_ref,
-    inc, acc, zmat, binv, load, pass_out, pass_in, staged, cut, slices, share_z, pat_in, pat0,
+    inc, acc, zmat, binv, load, pass_out, pass_in, staged, staged_more, cut, slices, share_z, pat_in, pat0,
     base_out, base, share, share_out, share_in, *rest,
 ):
-    mine, own, got = rest[:STEPS], rest[STEPS : 2 * STEPS], rest[2 * STEPS : 3 * STEPS]
+    mine, opposite, own, got = (rest[i * STEPS : (i + 1) * STEPS] for i in range(4))
     (
         local_sem, pass_ss, pass_rs, cut_ss, cut_rs, plane_ss, plane_rs, y_ss, y_rs, core_ss, core_rs,
-        slice_ss, slice_rs, pat_ss, pat_rs, base_ss, base_rs, share_ss, share_rs,
-    ) = rest[3 * STEPS :]
+        opp_ss, opp_rs, more_ss, more_rs, slice_ss, slice_rs, pat_ss, pat_rs, base_ss, base_rs, share_ss, share_rs,
+    ) = rest[4 * STEPS :]
     d, q = lax.axis_index("delay"), lax.axis_index("row")
     y, k = d // 2, d % 2
     x, z = q // NZ, q % NZ
     rows = PIECES * 16
     other = y * 2 + 1 - k
+    far = lax.rem(y + 2, NY) * 2 + k
     sent = []
 
     def remote(src, dst, ss, rs, dd, qq):
@@ -156,7 +157,7 @@
             out[0, part_of(i), :] = acc[1, part_of(i), :] + product(n, 0, i)
             return carry
 
-        lax.fori_loop(0, BLK, first, 0)
+        lax.fori_loop(0, BLK, first, 0, unroll=True)
         if n < STEPS - 1:
             pass_out[n + 1] = out[0].astype(BF16)
             pass_on(n + 1)
@@ -169,30 +170,44 @@
             out[1, part_of(i), :] = pass_in[n, part_of(i), :].astype(F32) + product(n, 1, i)
             return carry
 
-        lax.fori_loop(0, BLK, second, 0)
+        lax.fori_loop(0, BLK, second, 0, unroll=True)
         cur_ref[n] = got[n][:, pl.ds(SLOTS, BLK)].transpose(1, 0, 2, 3)
 
     chunks = [(SLOTS, BLK)] + [(lax.rem(x + a, NX) * GROUP, GROUP) for a in (0, 3, 1, 2)]
 
     def spread(n, j):
         here = pl.ds(*chunks[j])
-        for t, s in enumerate((2, 1, 3)):
+        for t, s in enumerate((1, 3)):
             remote(
                 own[n].at[here], got[n].at[d, here], y_ss.at[n, t], y_rs.at[n, t], lax.rem(y + s, NY) * 2 + k, q
             ).start()
 
+    def more(n):
+        arrived(opposite[n], opp_rs.at[n])
+        for t, p in enumerate(plane):
+            for c in range(CAP):
+                staged_more[n, t, c] = opposite[n][jnp.maximum(wanted[p, c, q], 0)]
+            remote(
+                staged_more.at[n, t], got[n].at[far, pl.ds(q * CAP, CAP)], more_ss.at[n], more_rs.at[n], d, p
+            ).start()
+        for c in range(CAP):
+            got[n][far, q * CAP + c] = opposite[n][jnp.maximum(wanted[q, c, q], 0)]
+        got[n][far, pl.ds(SLOTS, BLK)] = opposite[n][...]
+
     def across(n, e, t):
         src = own[n] if t == 3 else got[n].at[e]
         send(src, got[n].at[e], core_ss.at[n, t], core_rs.at[n, t], other, q)
 
     def hand_over(n):
-        for t, s in enumerate((2, 1, 3)):
+        for t, s in enumerate((1, 3)):
             e = lax.rem(y + NY - s, NY) * 2 + k
             arrived(got[n].at[e], y_rs.at[n, t])
             across(n, e, t)
+        arrived(got[n].at[far, pl.ds(0, SLOTS - CAP)], more_rs.at[n])
+        across(n, far, 2)
 
     def gathered(n):
-        for t, s in enumerate((2, 1, 3, 0)):
+        for t, s in enumerate((1, 3, 2, 0)):
             arrived(got[n].at[lax.rem(y + NY - s, NY) * 2 + 1 - k], core_rs.at[n, t])
 
     for n in range(STEPS):
@@ -228,6 +243,7 @@
         for c in range(CAP):
             own[n][q * CAP + c] = mine[n][jnp.maximum(wanted[q, c, q], 0)]
         own[n][pl.ds(SLOTS, BLK)] = mine[n][...]
+        send(mine[n], opposite[n], opp_ss.at[n], opp_rs.at[n], far, q)
 
         if n == 0:
             for m in range(2):
@@ -255,9 +271,13 @@
             copy = pltpu.make_async_copy(pat_in, pat0, local_sem.at[5])
             copy.start()
             copy.wait()
+        if n == 1:
+            for j in range(len(chunks)):
+                spread(n - 1, j)
         if n == STEPS - 1:
             gathered(n - 2)
             products(n - 2, acc)
+            more(n)
             spread(n, 0)
 
         for j, a in enumerate((0, 3, 1, 2), 1):
@@ -266,6 +286,8 @@
             arrived(own[n].at[there], plane_rs.at[n, from_x])
             if n == STEPS - 1:
                 spread(n, j)
+                if j == len(chunks) - 1:
+                    hand_over(n - 1)
         got[n][d] = own[n][...]
 
         if n < STEPS - 1:
@@ -292,10 +314,12 @@
                 send(share_out.at[n, e], share_in.at[n, d], share_ss.at[n, s], share_rs.at[n], e, q)
             if n == 0:
                 send_slices(1, [e for e in (4, 5, 3, 7) if e not in EARLY])
-            for j in range(len(chunks)):
-                spread(n, j)
+            if n == 1:
+                for j in range(len(chunks)):
+                    spread(n, j)
+            more(n)
         across(n, d, 3)
-        if n:
+        if n == 1:
             hand_over(n - 1)
 
     gathered(n - 1)
@@ -305,7 +329,8 @@
     products(n, fut_ref)
     for n in range(STEPS):
         left(staged.at[n], plane_ss.at[n])
-        for t in range(NY - 1):
+        left(staged_more.at[n], more_ss.at[n])
+        for t in range(2):
             left(own[n], y_ss.at[n, t])
     for copy, cond in sent:
         if cond is None:
@@ -338,6 +363,7 @@
             pltpu.VMEM((STEPS, rows, size), BF16),
             pltpu.VMEM((STEPS, rows, size), BF16),
             pltpu.VMEM((STEPS, OWNERS - 1, CAP, 16, size), BF16),
+            pltpu.VMEM((STEPS, OWNERS - 1, CAP, 16, size), BF16),
             pltpu.VMEM((PIECES, BLK, 16, size), BF16),
             pltpu.VMEM((2, PIECES, BLK, PICKS, 16, size), BF16),
             pltpu.VMEM((2, BLK, PICKS, 16, size), BF16),
@@ -348,15 +374,17 @@
             pltpu.VMEM((BLK, PIECES, 16, size), F32),
             pltpu.VMEM((STEPS - 1, PIECES, BLK, 16, size), BF16),
             pltpu.VMEM((STEPS - 1, PIECES, BLK, 16, size), BF16),
-            *[pltpu.VMEM((BLK, 16, size), BF16) for _ in range(STEPS)],
+            *[pltpu.VMEM((BLK, 16, size), BF16) for _ in range(2 * STEPS)],
             *[pltpu.VMEM((SLOTS + BLK, 16, size), BF16) for _ in range(STEPS)],
             *[pltpu.VMEM((PIECES, SLOTS + BLK, 16, size), BF16) for _ in range(STEPS)],
             dma((6,)),
             dma((STEPS,)), dma((STEPS,)),
             dma((PIECES,)), dma((1,)),
             dma((STEPS,)), dma((STEPS, NX)),
-            dma((STEPS, NY - 1)), dma((STEPS, NY - 1)),
+            dma((STEPS, 2)), dma((STEPS, 2)),
             dma((STEPS, NY)), dma((STEPS, NY)),
+            dma((STEPS,)), dma((STEPS,)),
+            dma((STEPS,)), dma((STEPS,)),
             dma((2, PIECES)), dma((2,)),
             dma((PIECES,)), dma((1,)),
             dma((2, PIECES)), dma((2,)),

time: 88.6 us -> 74.4 us (0.84)
  Pallas kernels: 86.2 us -> 72 us
    pallas_call x1, Pallas kernels: 86.2 us -> 72 us  [local(): pl.pallas_call(kernel, out_shape=(pltpu.VMEM((STEPS, BLK, PIECES, 16, siz...]
where the time goes in v4:
time: 74.4 us; the launch traced here: 74.2 us
  Pallas kernels  72 us (97%)
  local copies, waits for them, and re-layouts  1.54 us (2%)
    pallas_call x1, Pallas kernels, local(): pl.pallas_call(kernel, out_shape=(pltpu.VMEM((STEPS, BLK, PIECES, 16, siz...  72 us
    unnamed x2, local copies, waits for them, and re-layouts  1.54 us

profile of v4, /device:TPU:1, one launch (start us, length us, event | category | flops | bytes accessed | tf_op | source)
XLA Modules:
  0.0 74.2 jit_solution(11627013311112288323)
XLA Ops:
  0.6 72.0 %march.1 = (bf16[3,4,8,16,128]{4,3,2,1,0:T(8,128)(2,1)S(1)}, f32[2,512,128]{2,1,0:T(8,128)S(1)}) custom-call(bf16[3,512,128]{2,1,0:T(8,128)(2,1)} %inc_hbm.1, f32[2,512,128]{2,1,0:T(8,128)} %hist_hbm.1, bf16[2,512,2048]{2,1,0:T(8,128)(2,1)} %z_hbm.1, f32[4,128,128]{2,1,0:T(8,128)} %binv_hbm.1, s32[2,4,16]{2,1,0:T(4,128)} %pat.1, f32[4,128]{1,0:T(4,128)} %bitcast.5, ...), custom_call_target="tpu_custom_call" | custom-call | tf_op jit(solution)/shard_map/march/pallas_call | solution.py:349
  72.6 0.7 %copy.11 = bf16[3,512,128]{2,1,0:T(8,128)(2,1)} copy(bf16[3,512,128]{2,1,0:T(8,128)(2,1)S(1)} %bitcast.3) | data formatting | bytes 786432
  73.4 0.8 %copy.12 = f32[2,512,128]{2,1,0:T(8,128)} copy(f32[2,512,128]{2,1,0:T(8,128)S(1)} %get-tuple-element.7) | data formatting | bytes 1048576

commit v5 on v4

--- a/solution.py
+++ b/solution.py
@@ -69,7 +69,7 @@
     for start in loads:
         start.start()
 
-    around = [lax.rem(d + s, PIECES) for s in range(1, PIECES)]
+    around = [lax.rem(d + s, PIECES) for s in (4, 3, 5, 2, 6, 7, 1)]
     plane = [
         lax.rem(x + a, NX) * NZ + lax.rem(z + s, NZ) for a in (0, 1, 3, 2) for s in (4, 3, 5, 2, 6, 1, 7, 0) if a or s
     ]
@@ -212,7 +212,7 @@
 
     for n in range(STEPS):
         if n == 0:
-            for e in range(1, PIECES):
+            for e in (4, 5, 2, 3, 6, 7, 1):
                 send_if(d == 0, cut.at[e], mine[0], cut_ss.at[e], cut_rs.at[0], e, q)
             for e in range(1, PIECES):
                 send_if(d == 0, pat_hbm, pat_in, pat_ss.at[e], pat_rs.at[0], e, q)

time: 74.4 us -> 74 us (level)
  no operation moved by 1% of the time
where the time goes in v5:
time: 74 us; the launch traced here: 73.7 us
  Pallas kernels  71.6 us (97%)
  local copies, waits for them, and re-layouts  1.54 us (2%)
    pallas_call x1, Pallas kernels, local(): pl.pallas_call(kernel, out_shape=(pltpu.VMEM((STEPS, BLK, PIECES, 16, siz...  71.6 us
    unnamed x2, local copies, waits for them, and re-layouts  1.54 us

profile of v5, /device:TPU:1, one launch (start us, length us, event | category | flops | bytes accessed | tf_op | source)
XLA Modules:
  0.0 73.7 jit_solution(15268987557366151398)
XLA Ops:
  0.6 71.6 %march.1 = (bf16[3,4,8,16,128]{4,3,2,1,0:T(8,128)(2,1)S(1)}, f32[2,512,128]{2,1,0:T(8,128)S(1)}) custom-call(bf16[3,512,128]{2,1,0:T(8,128)(2,1)} %inc_hbm.1, f32[2,512,128]{2,1,0:T(8,128)} %hist_hbm.1, bf16[2,512,2048]{2,1,0:T(8,128)(2,1)} %z_hbm.1, f32[4,128,128]{2,1,0:T(8,128)} %binv_hbm.1, s32[2,4,16]{2,1,0:T(4,128)} %pat.1, f32[4,128]{1,0:T(4,128)} %bitcast.5, ...), custom_call_target="tpu_custom_call" | custom-call | tf_op jit(solution)/shard_map/march/pallas_call | solution.py:349
  72.2 0.7 %copy.11 = bf16[3,512,128]{2,1,0:T(8,128)(2,1)} copy(bf16[3,512,128]{2,1,0:T(8,128)(2,1)S(1)} %bitcast.3) | data formatting | bytes 786432
  73.0 0.8 %copy.12 = f32[2,512,128]{2,1,0:T(8,128)} copy(f32[2,512,128]{2,1,0:T(8,128)S(1)} %get-tuple-element.7) | data formatting | bytes 1048576
